TPU v7x, 128 devices: a whole 4x4x4 slice. The times are simulated.
128 devices in a mesh: queue: 64 (over x, y, z_lo, core), tok: 2 (over z_hi).
Axes of the slice: x: 4, y: 4, z: 4 (z_hi: 2, z_lo: 2; z = z_hi * 2 + z_lo), core: 2. Of those that a mesh axis runs over, the one named last changes fastest.
Arguments:
- latents: bfloat16 [64, 512, 3072], P('queue', 'tok'), may hold values from -5 to 5
- levels: int32 [64], P('queue'), may hold values from 0 to 63, as said below
- offsets: int32 [64], P('queue'), may hold values from 0 to 7
- level_table: float32 [64, 3, 3072], replicated, may hold values from -3 to 3
- w_qkv: bfloat16 [3072, 3, 1536], P(None, None, 'tok'), may hold values from -0.07252963 to 0.07252963
- w_out: bfloat16 [1536, 3072], P('tok'), may hold values from -0.15625 to 0.15625
- head_scale: float32 [12], P('tok'), may hold values from 2 to 24
Outputs:
- updated: bfloat16 [64, 512, 3072], P('queue', 'tok')
Inputs may be any that keep to these rules, and one draw needn't show every extreme that they name: levels never fall from one frame to the next; frame f has a level from f * 1 to f * 1 + max(1, 1); the first frame has level 0 and the last 63.
All inputs are finite; a program needn't handle non-finite values.
Results may differ from a plain program's by a relative error of at most 0.01.
Values may be sent and summed in bfloat16 or wider, within the bound.
A program may use at most 192 MiB of HBM per device.

v0:
```python
import jax
import jax.numpy as jnp
from jax import lax
from jax.sharding import PartitionSpec as P

DH = 128
WIN = 8


epsilon = 1e-06


def from_behind(array, axis, by):
    peers = lax.axis_size(axis)
    pairs = [(i, i + by) for i in range(peers) if 0 <= i + by < peers]
    return lax.ppermute(array, axis, pairs)


def rms_rows(values):
    return values * lax.rsqrt(jnp.mean(values * values, axis=-1, keepdims=True) + epsilon)


def attend_head(query_head, key_head, value_head, key_valid):
    scores = jnp.dot(query_head, key_head.T, preferred_element_type=jnp.float32)
    scores = jnp.where(key_valid[None, :], scores, -1e30)
    row_peak = jnp.max(scores, axis=1, keepdims=True)
    weights = jnp.exp(scores - row_peak)
    row_total = jnp.sum(weights, axis=1, keepdims=True)
    weighted = jnp.dot(weights.astype(jnp.bfloat16), value_head, preferred_element_type=jnp.float32)
    return weighted / row_total


def window_attention(query_rows, key_window, value_window, key_valid):

    def one_head(operands):
        return attend_head(operands[0], operands[1], operands[2], key_valid)

    result = lax.map(
        one_head,
        (
            jnp.moveaxis(query_rows, 1, 0),
            jnp.moveaxis(key_window, 1, 0),
            jnp.moveaxis(value_window, 1, 0),
        ),
    )
    result = jnp.moveaxis(result, 0, 1)
    return result.reshape(result.shape[0], -1).astype(jnp.bfloat16)


def shards(latents, levels, offsets, level_table, w_qkv, w_out, head_scale):
    latent_f = latents[0].astype(jnp.float32)
    modulation = lax.dynamic_index_in_dim(level_table, levels[0], 0, keepdims=False)
    normed = (rms_rows(latent_f) * (1.0 + modulation[1]) + modulation[0]).astype(jnp.bfloat16)
    local_heads = head_scale.shape[0]
    proj = jnp.einsum(
        "td,dkc->tkc",
        lax.all_gather(normed, "tok", axis=0, tiled=True),
        w_qkv,
        preferred_element_type=jnp.float32,
    )
    frame_tok = proj.shape[0]
    proj = proj.reshape(frame_tok, 3, local_heads, DH)
    queries = (rms_rows(proj[:, 0]) * head_scale[:, None] / jnp.sqrt(jnp.float32(DH))).astype(
        jnp.bfloat16
    )
    key_flat = rms_rows(proj[:, 1]).astype(jnp.bfloat16).reshape(frame_tok, local_heads * DH)
    value_flat = proj[:, 2].astype(jnp.bfloat16).reshape(frame_tok, local_heads * DH)
    kv_pair = jnp.stack([key_flat, value_flat])
    blocks = []
    for reach in range(-(WIN - 1), WIN):
        if reach == 0:
            blocks.append(kv_pair)
        else:
            blocks.append(from_behind(kv_pair, "queue", -reach))
    stacked = jnp.stack(blocks)
    offset_here = offsets[0]
    window = lax.dynamic_slice_in_dim(stacked, WIN - 1 - offset_here, WIN, 0)
    key_window = window[:, 0].reshape(WIN * frame_tok, local_heads, DH)
    value_window = window[:, 1].reshape(WIN * frame_tok, local_heads, DH)
    frame_index = lax.axis_index("queue")
    frames = lax.axis_size("queue")
    source = frame_index - offset_here + jnp.arange(WIN, dtype=jnp.int32)
    valid = (source >= 0) & (source < frames)
    key_valid = jnp.repeat(valid, frame_tok)
    attended = window_attention(queries, key_window, value_window, key_valid)
    branch = lax.psum_scatter(
        jnp.dot(attended, w_out, preferred_element_type=jnp.float32).astype(jnp.bfloat16),
        "tok",
        scatter_dimension=0,
        tiled=True,
    ).astype(jnp.float32)
    updated = (latent_f + modulation[2] * branch).astype(jnp.bfloat16)
    return updated[None]


def solution(mesh):
    placed = (
        P("queue", "tok", None),
        P("queue"),
        P("queue"),
        P(),
        P(None, None, "tok"),
        P("tok", None),
        P("tok"),
    )
    return jax.shard_map(
        shards, mesh=mesh, in_specs=placed, out_specs=P("queue", "tok", None), check_vma=False
    )
```

profile of v0, /device:TPU:1, one launch (start us, length us, event | category | flops | bytes accessed | tf_op | source)
XLA Modules:
  0.0 626.8 jit_solution(9757580978268865040)
XLA Ops:
  7.2 1.8 fusion.23
  10.0 3.1 fusion.26
  13.2 52.4 %all-gather.2.cloned.1.call-done = bf16[512,3072]{1,0:T(8,128)(2,1)} async-done(((bf16[256,3072]{1,0:T(8,128)(2,1)}), bf16[512,3072]{1,0:T(8,128)(2,1)}) %all-gather.2.cloned.1.call-update) | async-done | bytes 3145744 | tf_op jit(solution)/shard_map/all_gather | solution.py:57
  65.7 11.3 %fusion.28 = f32[512,3,768]{0,2,1:T(8,128)S(1)} fusion(bf16[3072,3,768]{2,0,1:T(8,128)(2,1)} %param.13, bf16[512,3072]{1,0:T(8,128)(2,1)} %all-gather.2.cloned.1.call-done), kind=kOutput, calls=%fused_computation.30 | convolution fusion | flops 7247757312 | bytes 22020096 | tf_op jit(solution)/shard_map/td,dkc->tkc/dot_general | solution.py:55
  77.7 1.7 pad_maximum_fusion
  79.6 5.3 collective-permute-start
  84.9 3.4 collective-permute-start.1
  88.3 4.0 collective-permute-start.2
  92.3 2.5 collective-permute-start.3
  95.5 2.9 collective-permute-start.4
  98.4 1.6 multiply_reduce_fusion.1
  100.0 19.4 %collective-permute-done = bf16[2,512,768]{1,2,0:T(8,128)(2,1)S(1)} collective-permute-done((bf16[2,512,768]{1,2,0:T(8,128)(2,1)}, bf16[2,512,768]{1,2,0:T(8,128)(2,1)S(1)}, u32[]{:S(2)}, u32[]{:S(2)}) %collective-permute-start) | collective-permute-done | bytes 1572896 | tf_op jit(solution)/shard_map/ppermute | solution.py:16
  120.6 1.6 collective-permute-start.5
  122.2 1.7 fusion.32
  123.9 29.3 %collective-permute-done.1 = bf16[2,512,768]{1,2,0:T(8,128)(2,1)} collective-permute-done((bf16[2,512,768]{1,2,0:T(8,128)(2,1)}, bf16[2,512,768]{1,2,0:T(8,128)(2,1)}, u32[]{:S(2)}, u32[]{:S(2)}) %collective-permute-start.1) | collective-permute-done | bytes 1572896 | tf_op jit(solution)/shard_map/ppermute | solution.py:16
  153.2 3.3 collective-permute-start.6
  156.4 2.7 bitcast_dynamic-update-slice_fusion.14
  159.1 27.7 %collective-permute-done.2 = bf16[2,512,768]{1,2,0:T(8,128)(2,1)} collective-permute-done((bf16[2,512,768]{1,2,0:T(8,128)(2,1)}, bf16[2,512,768]{1,2,0:T(8,128)(2,1)}, u32[]{:S(2)}, u32[]{:S(2)}) %collective-permute-start.2) | collective-permute-done | bytes 1572896 | tf_op jit(solution)/shard_map/ppermute | solution.py:16
  186.9 1.9 collective-permute-start.7
  188.8 2.7 bitcast_dynamic-update-slice_fusion.13
  191.4 27.7 %collective-permute-done.3 = bf16[2,512,768]{1,2,0:T(8,128)(2,1)} collective-permute-done((bf16[2,512,768]{1,2,0:T(8,128)(2,1)}, bf16[2,512,768]{1,2,0:T(8,128)(2,1)}, u32[]{:S(2)}, u32[]{:S(2)}) %collective-permute-start.3) | collective-permute-done | bytes 1572896 | tf_op jit(solution)/shard_map/ppermute | solution.py:16
  219.1 1.3 collective-permute-start.8
  220.4 2.7 bitcast_dynamic-update-slice_fusion.12
  223.0 2.7 bitcast_dynamic-update-slice_fusion.11
  225.7 10.2 %collective-permute-done.4 = bf16[2,512,768]{1,2,0:T(8,128)(2,1)S(1)} collective-permute-done((bf16[2,512,768]{1,2,0:T(8,128)(2,1)}, bf16[2,512,768]{1,2,0:T(8,128)(2,1)S(1)}, u32[]{:S(2)}, u32[]{:S(2)}) %collective-permute-start.4) | collective-permute-done | bytes 1572896 | tf_op jit(solution)/shard_map/ppermute | solution.py:16
  235.9 1.3 collective-permute-start.9
  238.5 1.3 collective-permute-start.10
  239.8 1.3 bitcast_dynamic-update-slice_fusion.9
  241.1 1.3 collective-permute-start.11
  243.7 1.3 collective-permute-start.12
  246.2 9.6 %collective-permute-done.8 = bf16[2,512,768]{1,2,0:T(8,128)(2,1)S(1)} collective-permute-done((bf16[2,512,768]{1,2,0:T(8,128)(2,1)}, bf16[2,512,768]{1,2,0:T(8,128)(2,1)S(1)}, u32[]{:S(2)}, u32[]{:S(2)}) %collective-permute-start.8) | collective-permute-done | bytes 1572896 | tf_op jit(solution)/shard_map/ppermute | solution.py:16
  255.8 1.5 collective-permute-start.13
  259.8 29.8 %collective-permute-done.9 = bf16[2,512,768]{1,2,0:T(8,128)(2,1)S(1)} collective-permute-done((bf16[2,512,768]{1,2,0:T(8,128)(2,1)}, bf16[2,512,768]{1,2,0:T(8,128)(2,1)S(1)}, u32[]{:S(2)}, u32[]{:S(2)}) %collective-permute-start.9) | collective-permute-done | bytes 1572896 | tf_op jit(solution)/shard_map/ppermute | solution.py:16
  290.9 45.9 %collective-permute-done.10 = bf16[2,512,768]{1,2,0:T(8,128)(2,1)S(1)} collective-permute-done((bf16[2,512,768]{1,2,0:T(8,128)(2,1)}, bf16[2,512,768]{1,2,0:T(8,128)(2,1)S(1)}, u32[]{:S(2)}, u32[]{:S(2)}) %collective-permute-start.10) | collective-permute-done | bytes 1572896 | tf_op jit(solution)/shard_map/ppermute | solution.py:16
  338.1 56.1 %collective-permute-done.11 = bf16[2,512,768]{1,2,0:T(8,128)(2,1)S(1)} collective-permute-done((bf16[2,512,768]{1,2,0:T(8,128)(2,1)}, bf16[2,512,768]{1,2,0:T(8,128)(2,1)S(1)}, u32[]{:S(2)}, u32[]{:S(2)}) %collective-permute-start.11) | collective-permute-done | bytes 1572896 | tf_op jit(solution)/shard_map/ppermute | solution.py:16
  396.7 2.8 collective-permute-done.13
  399.6 1.3 bitcast_dynamic-update-slice_fusion
  400.9 10.2 %constant_dynamic-slice_fusion.2 = (bf16[8,1,512,768]{2,3,1,0:T(8,128)(2,1)}, bf16[8,1,512,768]{2,3,1,0:T(8,128)(2,1)}) fusion(bf16[15,2,512,768]{2,3,1,0:T(8,128)(2,1)} %bitcast_dynamic-update-slice_fusion, s32[]{:T(128)S(6)} %select_n.12, s32[]{:T(128)S(6)} %add.89), kind=kLoop, calls=%fused_computation.63 | loop fusion | bytes 25165832 | tf_op jit(solution)/shard_map/slice | solution.py:79
  411.1 9.0 %copy.11 = bf16[8,1,512,768]{2,0,3,1:T(8,128)(2,1)} copy(bf16[8,1,512,768]{2,3,1,0:T(8,128)(2,1)} %get-tuple-element.74) | data formatting | bytes 12582912 | tf_op jit(solution)/shard_map/slice | solution.py:78
  420.1 10.4 %reshape_squeeze.6 = bf16[4096,6,128]{0,2,1:T(8,128)(2,1)} reshape(bf16[8,1,512,768]{2,0,3,1:T(8,128)(2,1)} %copy.11) | data formatting | bytes 12582912 | tf_op jit(solution)/shard_map/reshape;squeeze | solution.py:78
  430.5 8.9 %copy.12 = bf16[8,1,512,768]{2,0,3,1:T(8,128)(2,1)} copy(bf16[8,1,512,768]{2,3,1,0:T(8,128)(2,1)} %get-tuple-element.73) | data formatting | bytes 12582912 | tf_op jit(solution)/shard_map/slice | solution.py:79
  439.4 10.5 %reshape_squeeze.7 = bf16[4096,6,128]{0,2,1:T(8,128)(2,1)} reshape(bf16[8,1,512,768]{2,0,3,1:T(8,128)(2,1)} %copy.12) | data formatting | bytes 12582912 | tf_op jit(solution)/shard_map/reshape;squeeze | solution.py:79
  449.9 43.6 %while.11 = (s32[]{:T(128)}, bf16[6,512,128]{1,2,0:T(8,128)(2,1)S(1)}, bf16[6,512,128]{1,2,0:T(8,128)(2,1)S(1)}, bf16[6,4096,128]{1,2,0:T(8,128)(2,1)}, bf16[6,4...) while((s32[]{:T(128)}, bf16[6,512,128]{1,2,0:T(8,128)(2,1)S(1)}, ...), condition=%wide.region_6.7_spmd.clone, body=%wide.region_3.6_spmd.clone.sunk | while | flops 1090649088 | bytes 28085348 | solution.py:38
  450.0 2.6 select_reduce_fusion.2
  452.6 1.6 fusion.42
  454.3 2.8 fusion.43
  457.3 2.6 select_reduce_fusion.2
  459.9 1.6 fusion.42
  461.5 2.8 fusion.43
  464.5 2.6 select_reduce_fusion.2
  467.1 1.6 fusion.42
  468.8 2.8 fusion.43
  471.8 2.6 select_reduce_fusion.2
  474.4 1.6 fusion.42
  476.0 2.8 fusion.43
  479.1 2.6 select_reduce_fusion.2
  481.7 1.6 fusion.42
  483.3 2.8 fusion.43
  486.3 2.6 select_reduce_fusion.2
  488.9 1.6 fusion.42
  490.6 2.8 fusion.43
  493.5 6.4 %convolution_convert_fusion = bf16[512,3072]{1,0:T(8,128)(2,1)} fusion(bf16[512,768]{0,1:T(8,128)(2,1)S(1)} %bitcast.132, bf16[768,3072]{1,0:T(8,128)(2,1)} %param.14), kind=kOutput, calls=%fused_computation.24 | convolution fusion | flops 2417491968 | bytes 8650752 | tf_op jit(solution)/shard_map/dot_general | solution.py:87
  499.9 116.9 %reduce-scatter.2.cloned.1.call-done = bf16[256,3072]{1,0:T(8,128)(2,1)} async-done(((bf16[512,3072]{1,0:T(8,128)(2,1)}), bf16[256,3072]{1,0:T(8,128)(2,1)}) %reduce-scatter.2.cloned.1.call-update) | async-done | bytes 1572880 | tf_op jit(solution)/shard_map/reduce_scatter | solution.py:86
  616.8 3.1 fusion.30
  (60 shorter events, 15.9 us)
Async XLA Ops:
  6.5 59.1 %all-gather.2.cloned.1.call-start = ((), (), s32[]{:S(2)}) async-start(), calls=%async_computation.1 | async-start | bytes 4718592 | tf_op jit(solution)/shard_map/all_gather | solution.py:57
  13.2 603.6 %reduce-scatter.2.cloned.1.call-start = ((), (), s32[]{:S(2)}) async-start(), calls=%async_computation.2 | async-start | bytes 4718592 | tf_op jit(solution)/shard_map/reduce_scatter | solution.py:86
  77.0 2.6 copy-start.1
  77.4 44.7 %copy-start.3 = (f32[6]{0:T(128)S(1)}, f32[6]{0:T(128)}, u32[]{:S(2)}) copy-start(f32[6]{0:T(128)} %param.15) | copy-start | bytes 76
  79.6 39.8 %collective-permute-start = (bf16[2,512,768]{1,2,0:T(8,128)(2,1)}, bf16[2,512,768]{1,2,0:T(8,128)(2,1)S(1)}, u32[]{:S(2)}, u32[]{:S(2)}) collective-permute-start(bf16[2,512,768]{1,2,0:T(8,128)(2,1)} %pad_maximum_fusion), channel_id=1, source_target_pairs={{0,14},{2,16},{4,18},{6,20},{8,22},{10,24},{12,26},{14,28},{16,30}... | collective-permute-start | bytes 4718600 | tf_op jit(solution)/shard_map/ppermute | solution.py:16
  84.9 68.2 %collective-permute-start.1 = (bf16[2,512,768]{1,2,0:T(8,128)(2,1)}, bf16[2,512,768]{1,2,0:T(8,128)(2,1)}, u32[]{:S(2)}, u32[]{:S(2)}) collective-permute-start(bf16[2,512,768]{1,2,0:T(8,128)(2,1)} %pad_maximum_fusion), channel_id=1, source_target_pairs={{0,12},{2,14},{4,16},{6,18},{8,20},{10,22},{12,24},{14,26},{16,28}... | collective-permute-start | bytes 4718600 | tf_op jit(solution)/shard_map/ppermute | solution.py:16
  88.3 98.6 %collective-permute-start.2 = (bf16[2,512,768]{1,2,0:T(8,128)(2,1)}, bf16[2,512,768]{1,2,0:T(8,128)(2,1)}, u32[]{:S(2)}, u32[]{:S(2)}) collective-permute-start(bf16[2,512,768]{1,2,0:T(8,128)(2,1)} %pad_maximum_fusion), channel_id=1, source_target_pairs={{0,10},{2,12},{4,14},{6,16},{8,18},{10,20},{12,22},{14,24},{16,26}... | collective-permute-start | bytes 4718600 | tf_op jit(solution)/shard_map/ppermute | solution.py:16
  92.3 126.8 %collective-permute-start.3 = (bf16[2,512,768]{1,2,0:T(8,128)(2,1)}, bf16[2,512,768]{1,2,0:T(8,128)(2,1)}, u32[]{:S(2)}, u32[]{:S(2)}) collective-permute-start(bf16[2,512,768]{1,2,0:T(8,128)(2,1)} %pad_maximum_fusion), channel_id=1, source_target_pairs={{0,8},{2,10},{4,12},{6,14},{8,16},{10,18},{12,20},{14,22},{16,24},... | collective-permute-start | bytes 4718600 | tf_op jit(solution)/shard_map/ppermute | solution.py:16
  95.5 140.5 %collective-permute-start.4 = (bf16[2,512,768]{1,2,0:T(8,128)(2,1)}, bf16[2,512,768]{1,2,0:T(8,128)(2,1)S(1)}, u32[]{:S(2)}, u32[]{:S(2)}) collective-permute-start(bf16[2,512,768]{1,2,0:T(8,128)(2,1)} %pad_maximum_fusion), channel_id=1, source_target_pairs={{0,6},{2,8},{4,10},{6,12},{8,14},{10,16},{12,18},{14,20},{16,22},{... | collective-permute-start | bytes 4718600 | tf_op jit(solution)/shard_map/ppermute | solution.py:16
  119.4 1.2 copy-start.2
  120.6 117.9 %collective-permute-start.5 = (bf16[2,512,768]{1,2,0:T(8,128)(2,1)}, bf16[2,512,768]{1,2,0:T(8,128)(2,1)S(1)}, u32[]{:S(2)}, u32[]{:S(2)}) collective-permute-start(bf16[2,512,768]{1,2,0:T(8,128)(2,1)} %pad_maximum_fusion), channel_id=1, source_target_pairs={{0,4},{2,6},{4,8},{6,10},{8,12},{10,14},{12,16},{14,18},{16,20},{1... | collective-permute-start | bytes 4718600 | tf_op jit(solution)/shard_map/ppermute | solution.py:16
  153.2 88.0 %collective-permute-start.6 = (bf16[2,512,768]{1,2,0:T(8,128)(2,1)}, bf16[2,512,768]{1,2,0:T(8,128)(2,1)S(1)}, u32[]{:S(2)}, u32[]{:S(2)}) collective-permute-start(bf16[2,512,768]{1,2,0:T(8,128)(2,1)} %pad_maximum_fusion), channel_id=1, source_target_pairs={{0,2},{2,4},{4,6},{6,8},{8,10},{10,12},{12,14},{14,16},{16,18},{18... | collective-permute-start | bytes 4718600 | tf_op jit(solution)/shard_map/ppermute | solution.py:16
  186.9 56.8 %collective-permute-start.7 = (bf16[2,512,768]{1,2,0:T(8,128)(2,1)}, bf16[2,512,768]{1,2,0:T(8,128)(2,1)S(1)}, u32[]{:S(2)}, u32[]{:S(2)}) collective-permute-start(bf16[2,512,768]{1,2,0:T(8,128)(2,1)} %pad_maximum_fusion), channel_id=1, source_target_pairs={{2,0},{4,2},{6,4},{8,6},{10,8},{12,10},{14,12},{16,14},{18,16},{20... | collective-permute-start | bytes 4718600 | tf_op jit(solution)/shard_map/ppermute | solution.py:16
  219.1 36.7 %collective-permute-start.8 = (bf16[2,512,768]{1,2,0:T(8,128)(2,1)}, bf16[2,512,768]{1,2,0:T(8,128)(2,1)S(1)}, u32[]{:S(2)}, u32[]{:S(2)}) collective-permute-start(bf16[2,512,768]{1,2,0:T(8,128)(2,1)} %pad_maximum_fusion), channel_id=1, source_target_pairs={{4,0},{6,2},{8,4},{10,6},{12,8},{14,10},{16,12},{18,14},{20,16},{2... | collective-permute-start | bytes 4718600 | tf_op jit(solution)/shard_map/ppermute | solution.py:16
  235.9 53.7 %collective-permute-start.9 = (bf16[2,512,768]{1,2,0:T(8,128)(2,1)}, bf16[2,512,768]{1,2,0:T(8,128)(2,1)S(1)}, u32[]{:S(2)}, u32[]{:S(2)}) collective-permute-start(bf16[2,512,768]{1,2,0:T(8,128)(2,1)} %pad_maximum_fusion), channel_id=1, source_target_pairs={{6,0},{8,2},{10,4},{12,6},{14,8},{16,10},{18,12},{20,14},{22,16},{... | collective-permute-start | bytes 4718600 | tf_op jit(solution)/shard_map/ppermute | solution.py:16
  238.5 98.3 %collective-permute-start.10 = (bf16[2,512,768]{1,2,0:T(8,128)(2,1)}, bf16[2,512,768]{1,2,0:T(8,128)(2,1)S(1)}, u32[]{:S(2)}, u32[]{:S(2)}) collective-permute-start(bf16[2,512,768]{1,2,0:T(8,128)(2,1)} %pad_maximum_fusion), channel_id=1, source_target_pairs={{8,0},{10,2},{12,4},{14,6},{16,8},{18,10},{20,12},{22,14},{24,16},... | collective-permute-start | bytes 4718600 | tf_op jit(solution)/shard_map/ppermute | solution.py:16
  241.1 153.1 %collective-permute-start.11 = (bf16[2,512,768]{1,2,0:T(8,128)(2,1)}, bf16[2,512,768]{1,2,0:T(8,128)(2,1)S(1)}, u32[]{:S(2)}, u32[]{:S(2)}) collective-permute-start(bf16[2,512,768]{1,2,0:T(8,128)(2,1)} %pad_maximum_fusion), channel_id=1, source_target_pairs={{10,0},{12,2},{14,4},{16,6},{18,8},{20,10},{22,12},{24,14},{26,16}... | collective-permute-start | bytes 4718600 | tf_op jit(solution)/shard_map/ppermute | solution.py:16
  243.7 151.8 %collective-permute-start.12 = (bf16[2,512,768]{1,2,0:T(8,128)(2,1)}, bf16[2,512,768]{1,2,0:T(8,128)(2,1)S(1)}, u32[]{:S(2)}, u32[]{:S(2)}) collective-permute-start(bf16[2,512,768]{1,2,0:T(8,128)(2,1)} %pad_maximum_fusion), channel_id=1, source_target_pairs={{12,0},{14,2},{16,4},{18,6},{20,8},{22,10},{24,12},{26,14},{28,16}... | collective-permute-start | bytes 4718600 | tf_op jit(solution)/shard_map/ppermute | solution.py:16
  255.8 143.8 %collective-permute-start.13 = (bf16[2,512,768]{1,2,0:T(8,128)(2,1)}, bf16[2,512,768]{1,2,0:T(8,128)(2,1)S(1)}, u32[]{:S(2)}, u32[]{:S(2)}) collective-permute-start(bf16[2,512,768]{1,2,0:T(8,128)(2,1)} %pad_maximum_fusion), channel_id=1, source_target_pairs={{14,0},{16,2},{18,4},{20,6},{22,8},{24,10},{26,12},{28,14},{30,16}... | collective-permute-start | bytes 4718600 | tf_op jit(solution)/shard_map/ppermute | solution.py:16
  439.4 10.5 %copy-start.4 = (bf16[6,512,128]{1,2,0:T(8,128)(2,1)S(1)}, bf16[6,512,128]{1,2,0:T(8,128)(2,1)}, u32[]{:S(2)}) copy-start(bf16[6,512,128]{1,2,0:T(8,128)(2,1)} %custom-call.1) | copy-start | bytes 2359300
  499.9 116.9 %copy-start = (bf16[1,256,3072]{2,1,0:T(8,128)(2,1)S(1)}, bf16[1,256,3072]{2,1,0:T(8,128)(2,1)}, u32[]{:S(2)}) copy-start(bf16[1,256,3072]{2,1,0:T(8,128)(2,1)} %param.9) | copy-start | bytes 4718596
Sparse Core Ops, SparseCore 0:
  13.3 52.3 all-gather.1
  500.0 116.7 reduce-scatter.1
where the time goes:
time: 629 us; the launch traced here: 627 us
  waiting for transfers between devices  428 us (68%)
  local copies, waits for them, and re-layouts  75.3 us (12%)
  matrix products  49.9 us (8%)
  starting transfers between devices  32.7 us (5%)
  other arithmetic  25.8 us (4%)
  between operations  14.9 us (2%)
    ppermute x14, waiting for transfers between devices, from_behind(): return lax.ppermute(array, axis, pairs)  259 us
    reduce_scatter x1, waiting for transfers between devices, shards(): lax.psum_scatter(jnp.dot(attended, w_out, preferred_element_type=jnp.floa...  117 us
    all_gather x1, waiting for transfers between devices, shards(): lax.all_gather(normed, 'tok', axis=0, tiled=True)  52.4 us
    ppermute x14, starting transfers between devices, from_behind(): return lax.ppermute(array, axis, pairs)  32.7 us
    unnamed x23, local copies, waits for them, and re-layouts  23.6 us
    slice x2, local copies, waits for them, and re-layouts, shards(): value_window = window[:, 1].reshape(WIN * frame_tok, local_heads, DH)  19.2 us
    dot_general x6, matrix products, attend_head(): jnp.dot(weights.astype(jnp.bfloat16), value_head, preferred_element_type=...  16.6 us
    dot_general x6, matrix products, attend_head(): scores = jnp.dot(query_head, key_head.T, preferred_element_type=jnp.float32)  15.6 us
  transfers between devices with their start and end apart: 16, of which 12 were waited for; matrix products, arithmetic and copies ran while one was open for 4% of the time, Pallas kernels for 0%

commit v1 on v0

v1 whole, which is shorter than its diff:
```python
import functools

import jax
import jax.numpy as jnp
from jax import lax
from jax.experimental import pallas as pl
from jax.experimental.pallas import tpu as pltpu
from jax.sharding import PartitionSpec as P

D = 3072
DH = 128
WIN = 8
TOK = 512
HALF = 256
TRI = 384
COLS = 16
EPS = 1e-6
LOW = -1e30
HIGH = 1e30
WSUB = 4
MESH = pl.DeviceIdType.MESH
UP, DOWN = 0, 1
A, B, C1, D1, C2, D2 = range(6)


def body(
    x_ref, mod_ref, w_hbm, wo_hbm, off_ref, hs_ref,
    out_ref,
    near, far, qb, w_v, wo_v, nrm, st_kv, st_q, scores, acc_s, m_s, l_s, att, ob, offs,
    w_sem, off_sem, cut_s, cut_r, inkv_s, inkv_r, inq_s, inq_r, y_s, y_r, f_s, f_r,
    c0_s, c0_r, c1_s, c1_r, c2_s, c2_r, wc_s, wc_r, wi_s, wi_r, wk_s, wk_r, wj_s, wj_r, o_s, o_r,
):
    q = lax.axis_index("queue")
    t = lax.axis_index("tok")
    core = lax.rem(q, 2)
    zlo = lax.rem(q // 2, 2)
    col = q // 4
    inner_q = q + 2 - 4 * zlo
    inner = (inner_q, t)
    cut = (inner_q, 1 - t)
    peer = (q, 1 - t)
    other = (q + 1 - 2 * core, t)
    upper = (q + 4, t)
    lower = (q - 4, t)
    has_up, has_low = col < COLS - 1, col > 0
    pending = []

    def send(src, dst, s_sem, r_sem, to, when=None):
        copy = pltpu.make_async_remote_copy(
            src_ref=src, dst_ref=dst, send_sem=s_sem, recv_sem=r_sem, device_id=to, device_id_type=MESH
        )
        pending.append((copy, when))
        if when is None:
            copy.start()
        else:
            pl.when(when)(copy.start)

    def recv(dst, s_sem, r_sem, to, when=None):
        copy = pltpu.make_async_remote_copy(
            src_ref=dst, dst_ref=dst, send_sem=s_sem, recv_sem=r_sem, device_id=to, device_id_type=MESH
        )
        if when is None:
            copy.wait_recv()
        else:
            pl.when(when)(copy.wait_recv)

    loads = [
        pltpu.make_async_copy(w_hbm.at[i], w_v.at[i], w_sem.at[i]) for i in range(3)
    ]
    for i in (1, 2, 0):
        loads[i].start()
    wo_load = pltpu.make_async_copy(
        wo_hbm, wo_v.at[pl.ds(pl.multiple_of(t * 768, 768), 768)], w_sem.at[3]
    )
    wo_load.start()

    barrier = pltpu.get_barrier_semaphore()
    for to in (inner, cut, peer, other):
        pl.semaphore_signal(barrier, inc=1, device_id=to, device_id_type=MESH)

    @pl.when(has_up)
    def _():
        pl.semaphore_signal(barrier, inc=1, device_id=upper, device_id_type=MESH)

    @pl.when(has_low)
    def _():
        pl.semaphore_signal(barrier, inc=1, device_id=lower, device_id_type=MESH)

    def normalize(r):
        rows = pl.ds(r * 128, 128)
        x = x_ref[0, rows, :].astype(jnp.float32)
        inv = lax.rsqrt(jnp.mean(x * x, axis=-1, keepdims=True) + EPS)
        nrm[0, rows, :] = (x * inv * (1.0 + mod_ref[1:2, :]) + mod_ref[0:1, :]).astype(jnp.bfloat16)

    def send_normed(r):
        rows = pl.ds(r * 128, 128)
        send(nrm.at[0, rows], nrm.at[1, rows], cut_s.at[r], cut_r.at[r], cut)

    normalize(0)
    pl.semaphore_wait(barrier, 4 + jnp.where(has_up, 1, 0) + jnp.where(has_low, 1, 0))
    send_normed(0)
    normalize(1)
    send_normed(1)
    send(off_ref, offs, off_sem.at[0], off_sem.at[1], inner)

    slot_of = {A: zlo, B: 1 - zlo, C1: 1 - zlo, D1: zlo, C2: 1 - zlo, D2: zlo}
    own0 = pl.multiple_of(t * HALF, HALF)
    frn0 = pl.multiple_of((1 - t) * HALF, HALF)
    rows_of = {
        A: pl.ds(own0, 256), B: pl.ds(own0, 256),
        C1: pl.ds(frn0, 128), D1: pl.ds(frn0, 128),
        C2: pl.ds(pl.multiple_of(frn0 + 128, 128), 128), D2: pl.ds(pl.multiple_of(frn0 + 128, 128), 128),
    }

    def frame(piece, of_core=core):
        return of_core + 2 * slot_of[piece]

    def near_at(side, piece, of_core=core):
        return near.at[side, frame(piece, of_core), :, rows_of[piece], :]

    def far_at(side, piece, of_core=core):
        return far.at[side, frame(piece, of_core), :, rows_of[piece], :]

    def project(part, nslot, src0, rows, piece):
        st_rows = pl.ds((0, 256, 384)[part], rows)
        for mat in (1, 2, 0):
            if part == 0:
                loads[mat].wait()
            y = jnp.dot(
                nrm[nslot, src0 : src0 + rows, :], w_v[mat], preferred_element_type=jnp.float32
            )
            thirds = []
            for h in range(6):
                yh = y[:, h * DH : (h + 1) * DH]
                if mat != 2:
                    yh = yh * lax.rsqrt(jnp.mean(yh * yh, axis=-1, keepdims=True) + EPS)
                if mat == 0:
                    yh = yh * hs_ref[h] * (DH ** -0.5)
                thirds.append(yh.astype(jnp.bfloat16))
            for h in range(3):
                lanes = slice(h * DH, (h + 1) * DH)
                mine = jnp.where(zlo == 0, thirds[h], thirds[h + 3])
                theirs = jnp.where(zlo == 0, thirds[h + 3], thirds[h])
                if mat == 0:
                    qb[slot_of[piece], rows_of[piece], lanes] = mine
                    st_q[st_rows, lanes] = theirs
                else:
                    far[0, frame(piece), mat - 1, rows_of[piece], lanes] = mine
                    st_kv[mat - 1, st_rows, lanes] = theirs
            if mat == 2:
                send(st_kv.at[:, st_rows], far_at(0, piece), inkv_s.at[part], inkv_r.at[part], inner)
                spread(piece)
            if mat == 0:
                send(
                    st_q.at[st_rows], qb.at[slot_of[piece], rows_of[piece]],
                    inq_s.at[part], inq_r.at[part], inner,
                )

    def spread(piece):
        send(far_at(0, piece), near_at(1, piece), y_s.at[UP, piece], y_r.at[UP, piece], upper, has_up)
        send(far_at(0, piece), near_at(0, piece), y_s.at[DOWN, piece], y_r.at[DOWN, piece], lower, has_low)
        send(far_at(0, piece), far_at(0, piece), c0_s.at[piece], c0_r.at[piece], other)

    def from_inner(part, piece):
        recv(far_at(0, piece), inkv_s.at[part], inkv_r.at[part], inner)
        spread(piece)

    def pass_on(piece):
        recv(near_at(1, piece), y_s.at[UP, piece], y_r.at[UP, piece], upper, has_low)
        send(
            near_at(1, piece), far_at(2, piece), f_s.at[UP, piece], f_r.at[UP, piece], upper,
            has_up & has_low & (frame(piece) >= 1),
        )
        send(near_at(1, piece), near_at(1, piece), c1_s.at[UP, piece], c1_r.at[UP, piece], other, has_low)
        recv(near_at(0, piece), y_s.at[DOWN, piece], y_r.at[DOWN, piece], lower, has_up)
        send(
            near_at(0, piece), far_at(1, piece), f_s.at[DOWN, piece], f_r.at[DOWN, piece], lower,
            has_up & has_low & (frame(piece) <= 2),
        )
        send(near_at(0, piece), near_at(0, piece), c1_s.at[DOWN, piece], c1_r.at[DOWN, piece], other, has_up)

    from_up2, from_low2 = col < COLS - 2, col > 1

    def share_far(piece):
        when = from_low2 & (frame(piece) >= 1)
        recv(far_at(2, piece), f_s.at[UP, piece], f_r.at[UP, piece], upper, when)
        send(far_at(2, piece), far_at(2, piece), c2_s.at[UP, piece], c2_r.at[UP, piece], other, when)
        when = from_up2 & (frame(piece) <= 2)
        recv(far_at(1, piece), f_s.at[DOWN, piece], f_r.at[DOWN, piece], lower, when)
        send(far_at(1, piece), far_at(1, piece), c2_s.at[DOWN, piece], c2_r.at[DOWN, piece], other, when)

    j = core + 2 * zlo
    w_rows = 192 // WSUB

    def quarter(half, which, sub):
        return pl.ds(pl.multiple_of(half * 768 + which * 192 + sub * w_rows, 16), w_rows)

    other_j, inner_j = j + 1 - 2 * core, j + 2 - 4 * zlo
    diag_j = 3 - j

    def wo_cut(sub):
        src = pl.ds(pl.multiple_of(inner_j * 192 + sub * w_rows, 16), w_rows)
        send(wo_hbm.at[src], wo_v.at[quarter(t, inner_j, sub)], wc_s.at[sub], wc_r.at[sub], cut)

    def wo_share(sub):
        mine = wo_v.at[quarter(1 - t, j, sub)]
        recv(mine, wc_s.at[sub], wc_r.at[sub], cut)
        send(mine, mine, wi_s.at[sub], wi_r.at[sub], inner)
        send(mine, mine, wk_s.at[sub], wk_r.at[sub], other)

    def wo_second(sub):
        theirs = wo_v.at[quarter(1 - t, inner_j, sub)]
        recv(theirs, wi_s.at[sub], wi_r.at[sub], inner)
        send(theirs, theirs, wj_s.at[sub], wj_r.at[sub], other)

    def wo_last(sub):
        recv(wo_v.at[quarter(1 - t, other_j, sub)], wk_s.at[sub], wk_r.at[sub], other)
        recv(wo_v.at[quarter(1 - t, diag_j, sub)], wj_s.at[sub], wj_r.at[sub], other)

    project(0, 0, 0, 256, A)

    @pl.when(col == COLS - 1)
    def _():
        near[0] = jnp.zeros_like(near[0])

    @pl.when(col == 0)
    def _():
        near[1] = jnp.zeros_like(near[1])

    @pl.when(col >= COLS - 2)
    def _():
        far[1] = jnp.zeros_like(far[1])

    @pl.when(col <= 1)
    def _():
        far[2] = jnp.zeros_like(far[2])

    from_inner(0, B)
    pass_on(A)
    recv(nrm.at[1, pl.ds(0, 128)], cut_s.at[0], cut_r.at[0], cut)
    project(1, 1, 0, 128, C1)
    pass_on(B)
    from_inner(1, D1)
    recv(nrm.at[1, pl.ds(128, 128)], cut_s.at[1], cut_r.at[1], cut)
    for sub in range(WSUB):
        wo_cut(sub)
    project(2, 1, 128, 128, C2)
    pass_on(C1)
    pass_on(D1)
    from_inner(2, D2)
    wo_share(0)
    pass_on(C2)
    pass_on(D2)
    wo_share(1)

    recv(offs, off_sem.at[0], off_sem.at[1], inner)
    for part, piece in ((0, B), (1, D1), (2, D2)):
        recv(qb.at[slot_of[piece], rows_of[piece]], inq_s.at[part], inq_r.at[part], inner)
    for piece in range(6):
        recv(near_at(1, piece, 1 - core), c1_s.at[UP, piece], c1_r.at[UP, piece], other, has_low)
        recv(near_at(0, piece, 1 - core), c1_s.at[DOWN, piece], c1_r.at[DOWN, piece], other, has_up)

    def offset_of(slot):
        return jnp.where(slot == zlo, off_ref[0], offs[0])

    def attend(slot, half, h, blocks, first):
        lanes = pl.ds(pl.multiple_of(h * DH, DH), DH)
        rows = pl.ds(pl.multiple_of(half * HALF, HALF), HALF)
        place = (slot * 2 + half) * 3 + h
        queries = qb[slot, rows, lanes]
        peak = None
        for b, (ref, lead, valid) in enumerate(blocks):
            keys = ref[(*lead, 0, slice(None), lanes)]
            s = lax.dot_general(
                queries, keys, (((1,), (1,)), ((), ())), preferred_element_type=jnp.float32
            )
            scores[:, b * TOK : (b + 1) * TOK] = s
            top = jnp.max(s, axis=1, keepdims=True)
            if valid is not None:
                top = jnp.where(valid, top, LOW)
            peak = top if peak is None else jnp.maximum(peak, top)
        if not first:
            before = m_s[place][:, :1]
            peak = jnp.maximum(peak, before)
        total = None
        weighted = None
        for b, (ref, lead, valid) in enumerate(blocks):
            base = peak if valid is None else jnp.where(valid, peak, HIGH)
            p = jnp.exp(scores[:, b * TOK : (b + 1) * TOK] - base)
            part = jnp.sum(p, axis=1, keepdims=True)
            values = ref[(*lead, 1, slice(None), lanes)]
            o = jnp.dot(p.astype(jnp.bfloat16), values, preferred_element_type=jnp.float32)
            total = part if total is None else total + part
            weighted = o if weighted is None else weighted + o
        if first:
            m_s[place] = jnp.broadcast_to(peak, (HALF, DH))
            l_s[place] = jnp.broadcast_to(total, (HALF, DH))
            acc_s[place] = weighted
        else:
            scale = jnp.exp(before - peak)
            total = total + l_s[place][:, :1] * scale
            weighted = weighted + acc_s[place] * scale
            ob[slot, rows, lanes] = (weighted / total).astype(jnp.bfloat16)

    def stage_near(slot, half, h):
        mine = core + 2 * slot
        o = offset_of(slot)
        blocks = [(far, (0, mine), None)]
        for i in range(4):
            below = 4 + i - mine > WIN - 1 - o
            side = jnp.where(below, 1, 0)
            valid = jnp.where(below, has_low, has_up)
            blocks.append((near, (side, i), valid))
        attend(slot, half, h, blocks, True)

    def stage_far(slot, half, h):
        mine = core + 2 * slot
        o = offset_of(slot)
        blocks = []
        for n in range(3):
            r = n + jnp.where(n >= mine, 1, 0)
            less = r < mine
            inside = jnp.where(less, mine - r <= o, r - mine <= WIN - 1 - o)
            side = jnp.where(inside, 0, jnp.where(less, 1, 2))
            valid = inside | jnp.where(less, from_up2, from_low2)
            blocks.append((far, (side, r), valid))
        attend(slot, half, h, blocks, False)

    def near_loop(i, carry):
        stage_near(i // 6, lax.rem(i // 3, 2), lax.rem(i, 3))
        return carry

    lax.fori_loop(0, 6, near_loop, 0)
    wo_share(2)
    wo_second(0)
    lax.fori_loop(6, 12, near_loop, 0)
    wo_share(3)
    wo_second(1)

    for piece in range(6):
        share_far(piece)
    wo_second(2)
    wo_second(3)
    for piece in range(6):
        recv(far_at(0, piece, 1 - core), c0_s.at[piece], c0_r.at[piece], other)
        recv(
            far_at(2, piece, 1 - core), c2_s.at[UP, piece], c2_r.at[UP, piece], other,
            from_low2 & (frame(piece, 1 - core) >= 1),
        )
        recv(
            far_at(1, piece, 1 - core), c2_s.at[DOWN, piece], c2_r.at[DOWN, piece], other,
            from_up2 & (frame(piece, 1 - core) <= 2),
        )

    def att_at(triple):
        return att.at[:, pl.ds(pl.multiple_of(triple * TRI, 128), TRI)]

    triple = 2 * t + zlo
    for n, (slot, half, to) in enumerate(
        ((1 - zlo, 1 - t, cut), (1 - zlo, t, inner), (zlo, 1 - t, peer), (zlo, t, None))
    ):
        lax.fori_loop(0, 3, lambda h, carry: (stage_far(slot, half, h), carry)[1], 0)
        rows = pl.ds(pl.multiple_of(half * HALF, HALF), HALF)
        if to is None:
            for h in range(3):
                att[:, pl.ds(pl.multiple_of(triple * TRI + h * DH, 128), DH)] = ob[slot, rows, h * DH : (h + 1) * DH]
        else:
            send(ob.at[slot, rows], att_at(triple), o_s.at[n], o_r.at[n], to)

    wo_load.wait()
    for sub in range(WSUB):
        wo_last(sub)
    for n, (from_t, from_z, to) in enumerate(((1 - t, 1 - zlo, cut), (t, 1 - zlo, inner), (1 - t, zlo, peer))):
        recv(att_at(2 * from_t + from_z), o_s.at[n], o_r.at[n], to)

    def out_tile(n, carry):
        lanes = pl.ds(pl.multiple_of(n * 512, 512), 512)
        branch = jnp.dot(att[...], wo_v[:, lanes], preferred_element_type=jnp.float32)
        x = x_ref[0, :, lanes].astype(jnp.float32)
        out_ref[0, :, lanes] = (x + mod_ref[2:3, lanes] * branch).astype(jnp.bfloat16)
        return carry

    lax.fori_loop(0, D // 512, out_tile, 0)
    for copy, when in pending:
        if when is None:
            copy.wait_send()
        else:
            pl.when(when)(copy.wait_send)


def shards(latents, levels, offsets, level_table, w_qkv, w_out, head_scale):
    table = jnp.transpose(level_table, (1, 0, 2))
    modulation = lax.dynamic_index_in_dim(table, levels[0], 1, keepdims=False)
    weights = jnp.transpose(w_qkv, (1, 0, 2))
    bf, f32 = jnp.bfloat16, jnp.float32
    dma = pltpu.SemaphoreType.DMA
    vmem = pl.BlockSpec(memory_space=pltpu.VMEM)
    smem = pl.BlockSpec(memory_space=pltpu.SMEM)
    hbm = pl.BlockSpec(memory_space=pl.ANY)
    pair = lambda *n: [dma(n), dma(n)]
    return pl.pallas_call(
        body,
        out_shape=jax.ShapeDtypeStruct((1, HALF, D), bf),
        in_specs=[vmem, vmem, hbm, hbm, smem, smem],
        out_specs=vmem,
        scratch_shapes=[
            pltpu.VMEM((2, 4, 2, TOK, TRI), bf),
            pltpu.VMEM((3, 4, 2, TOK, TRI), bf),
            pltpu.VMEM((2, TOK, TRI), bf),
            pltpu.VMEM((3, D, 768), bf),
            pltpu.VMEM((1536, D), bf),
            pltpu.VMEM((2, HALF, D), bf),
            pltpu.VMEM((2, TOK, TRI), bf),
            pltpu.VMEM((TOK, TRI), bf),
            pltpu.VMEM((HALF, 5 * TOK), f32),
            pltpu.VMEM((12, HALF, DH), f32),
            pltpu.VMEM((12, HALF, DH), f32),
            pltpu.VMEM((12, HALF, DH), f32),
            pltpu.VMEM((HALF, 1536), bf),
            pltpu.VMEM((2, TOK, TRI), bf),
            pltpu.SMEM((1,), jnp.int32),
            dma((4,)), dma((2,)),
            *pair(2), *pair(3), *pair(3), *pair(2, 6), *pair(2, 6),
            *pair(6), *pair(2, 6), *pair(2, 6),
            *pair(WSUB), *pair(WSUB), *pair(WSUB), *pair(WSUB), *pair(3),
        ],
        compiler_params=pltpu.CompilerParams(
            collective_id=0, has_side_effects=True, vmem_limit_bytes=62 * 2**20
        ),
        cost_estimate=pl.CostEstimate(flops=17 * 10**9, bytes_accessed=25 * 10**6, transcendentals=13 * 10**6),
        name="frame_attention",
    )(latents, modulation, weights, w_out, offsets, head_scale)


def solution(mesh):
    placed = (
        P("queue", "tok", None),
        P("queue"),
        P("queue"),
        P(),
        P(None, None, "tok"),
        P("tok", None),
        P("tok"),
    )
    return jax.shard_map(
        shards, mesh=mesh, in_specs=placed, out_specs=P("queue", "tok", None), check_vma=False
    )
```

time: 629 us -> 121 us (0.19)
  waiting for transfers between devices: 428 us -> 0 us
  Pallas kernels: 0 us -> 116 us
  local copies, waits for them, and re-layouts: 75.3 us -> 4.28 us
  matrix products: 49.9 us -> 0 us
  starting transfers between devices: 32.7 us -> 0 us
  other arithmetic: 25.8 us -> 0 us
  between operations: 14.9 us -> 1.31 us
    ppermute x14 -> x0, waiting for transfers between devices: 259 us -> none  [from_behind(): return lax.ppermute(array, axis, pairs)]
    reduce_scatter x1 -> x0, waiting for transfers between devices: 117 us -> none  [shards(): lax.psum_scatter(jnp.dot(attended, w_out, preferred_element_type=jnp.floa...]
    pallas_call x0 -> x1, Pallas kernels: none -> 116 us  [shards(): pl.pallas_call(body, out_shape=jax.ShapeDtypeStruct((1, HALF, D), bf), in...]
    all_gather x1 -> x0, waiting for transfers between devices: 52.4 us -> none  [shards(): lax.all_gather(normed, 'tok', axis=0, tiled=True)]
    dot_general x14 -> x0, matrix products: 49.9 us -> none  [the longest x6 16.6 us: attend_head(): jnp.dot(weights.astype(jnp.bfloat16), value_head, preferred_element_type=...]
    ppermute x14 -> x0, starting transfers between devices: 32.7 us -> none  [from_behind(): return lax.ppermute(array, axis, pairs)]
    slice x4 -> x0, local copies, waits for them, and re-layouts: 28.2 us -> none  [the longest x2 19.2 us: shards(): value_window = window[:, 1].reshape(WIN * frame_tok, local_heads, DH)]
    another operation x3 -> x1, local copies, waits for them, and re-layouts: 22.2 us -> 0.99 us  [the longest x1 10.5 us: shards(): value_window = window[:, 1].reshape(WIN * frame_tok, local_heads, DH)]
  transfers between devices with their start and end apart: 16 -> 0, of which waited for: 12 -> 0; matrix products, arithmetic and copies ran while one was open for 4% -> 0% of each run, Pallas kernels for 0% -> 0%
where the time goes in v1:
time: 121 us
  Pallas kernels  116 us (96%)
  local copies, waits for them, and re-layouts  4.28 us (4%)
  between operations  1.31 us (1%)
    pallas_call x1, Pallas kernels, shards(): pl.pallas_call(body, out_shape=jax.ShapeDtypeStruct((1, HALF, D), bf), in...  116 us
    unnamed x2, local copies, waits for them, and re-layouts  3.29 us

profile of v1, /device:TPU:1, one launch (start us, length us, event | category | flops | bytes accessed | tf_op | source)
XLA Modules:
  0.0 121.2 jit_solution(13253463832549751642)
XLA Ops:
  1.3 1.0 constant_dynamic-slice_fusion
  2.3 0.6 copy.10
  2.9 115.6 %frame_attention.1 = bf16[1,256,3072]{2,1,0:T(8,128)(2,1)} custom-call(bf16[1,256,3072]{2,1,0:T(8,128)(2,1)} %x_ref.1, f32[3,3072]{1,0:T(4,128)} %bitcast.8, bf16[3,3072,768]{2,1,0:T(8,128)(2,1)} %bitcast.9, bf16[768,3072]{1,0:T(8,128)(2,1)} %wo_hbm.1, s32[1]{0:T(128)S(6)} %copy.13.off_ref, f32[6]{0:T(128)} %hs_ref.1), custom_call_target="tpu_custom_call" | custom-call | flops 16999999488 | bytes 25000000 | tf_op jit(solution)/shard_map/frame_attention/pallas_call | solution.py:401
  118.6 2.7 %copy.14 = bf16[1,256,3072]{2,1,0:T(8,128)(2,1)} copy(bf16[1,256,3072]{2,1,0:T(8,128)(2,1)} %frame_attention.1) | data formatting | bytes 3145728

commit v2 on v1

v2 whole, which is shorter than its diff:
```python
import functools

import jax
import jax.numpy as jnp
from jax import lax
from jax.experimental import pallas as pl
from jax.experimental.pallas import tpu as pltpu
from jax.sharding import PartitionSpec as P

D = 3072
DH = 128
WIN = 8
TOK = 512
HALF = 256
TRI = 384
COLS = 16
EPS = 1e-6
LOW = -1e30
HIGH = 1e30
WSUB = 4
MESH = pl.DeviceIdType.MESH
UP, DOWN = 0, 1
A, B, C1, D1, C2, D2 = range(6)


def body(
    x_ref, mod_ref, w_hbm, wo_hbm, off_ref, hs_ref,
    out_ref,
    near_a, near_c, far_a, far_c, qb, w_v, wo_v, nrm, st_kv, st_q, even, odd, acc_s, m_s, l_s, att, ob, offs,
    w_sem, off_sem, cut_s, cut_r, inkv_s, inkv_r, inq_s, inq_r, y_s, y_r, f_s, f_r,
    c0_s, c0_r, c1_s, c1_r, c2_s, c2_r, wc_s, wc_r, wi_s, wi_r, wk_s, wk_r, wj_s, wj_r, o_s, o_r,
):
    q = lax.axis_index("queue")
    t = lax.axis_index("tok")
    core = lax.rem(q, 2)
    zlo = lax.rem(q // 2, 2)
    col = q // 4
    inner_q = q + 2 - 4 * zlo
    inner = (inner_q, t)
    cut = (inner_q, 1 - t)
    peer = (q, 1 - t)
    other = (q + 1 - 2 * core, t)
    upper = (q + 4, t)
    lower = (q - 4, t)
    has_up, has_low = col < COLS - 1, col > 0
    pending = []

    def send(src, dst, s_sem, r_sem, to, when=None):
        copy = pltpu.make_async_remote_copy(
            src_ref=src, dst_ref=dst, send_sem=s_sem, recv_sem=r_sem, device_id=to, device_id_type=MESH
        )
        pending.append((copy, when))
        if when is None:
            copy.start()
        else:
            pl.when(when)(copy.start)

    def recv(dst, s_sem, r_sem, to, when=None):
        copy = pltpu.make_async_remote_copy(
            src_ref=dst, dst_ref=dst, send_sem=s_sem, recv_sem=r_sem, device_id=to, device_id_type=MESH
        )
        if when is None:
            copy.wait_recv()
        else:
            pl.when(when)(copy.wait_recv)

    loads = [
        pltpu.make_async_copy(w_hbm.at[i], w_v.at[i], w_sem.at[i]) for i in range(3)
    ]
    loads[1].start()
    loads[2].start()
    wo_load = pltpu.make_async_copy(
        wo_hbm, wo_v.at[pl.ds(pl.multiple_of(t * 768, 768), 768)], w_sem.at[3]
    )

    barrier = pltpu.get_barrier_semaphore()
    for to in (inner, cut, peer, other):
        pl.semaphore_signal(barrier, inc=1, device_id=to, device_id_type=MESH)

    @pl.when(has_up)
    def _():
        pl.semaphore_signal(barrier, inc=1, device_id=upper, device_id_type=MESH)

    @pl.when(has_low)
    def _():
        pl.semaphore_signal(barrier, inc=1, device_id=lower, device_id_type=MESH)

    def normalize(r):
        rows = pl.ds(r * 128, 128)
        x = x_ref[0, rows, :].astype(jnp.float32)
        inv = lax.rsqrt(jnp.mean(x * x, axis=-1, keepdims=True) + EPS)
        nrm[0, rows, :] = (x * inv * (1.0 + mod_ref[1:2, :]) + mod_ref[0:1, :]).astype(jnp.bfloat16)

    def send_normed(r):
        rows = pl.ds(r * 128, 128)
        send(nrm.at[0, rows], nrm.at[1, rows], cut_s.at[r], cut_r.at[r], cut)

    normalize(0)
    pl.semaphore_wait(barrier, 4 + jnp.where(has_up, 1, 0) + jnp.where(has_low, 1, 0))
    send_normed(0)
    normalize(1)
    first_normed = pending.pop()[0]
    send(off_ref, offs, off_sem.at[0], off_sem.at[1], inner)

    slot_of = {A: zlo, B: 1 - zlo, C1: 1 - zlo, D1: zlo, C2: 1 - zlo, D2: zlo}
    group_of = {A: 3, B: 0, C1: 1, D1: 2, C2: 1, D2: 2}
    rows_of = {
        A: pl.ds(0, 256), B: pl.ds(0, 256), C1: pl.ds(0, 128), D1: pl.ds(0, 128),
        C2: pl.ds(128, 128), D2: pl.ds(128, 128),
    }

    def frame(piece, of_core=core):
        return of_core + 2 * slot_of[piece]

    def near_at(side, piece, of_core=core):
        ref = near_a if piece in (A, B) else near_c
        return ref.at[side, frame(piece, of_core), :, rows_of[piece], :]

    def far_at(side, piece, of_core=core):
        ref = far_a if piece in (A, B) else far_c
        return ref.at[side, frame(piece, of_core), :, rows_of[piece], :]

    def q_at(piece):
        return qb.at[group_of[piece], rows_of[piece], :]

    def project(part, nslot, src0, rows, piece):
        st_rows = pl.ds((0, 256, 384)[part], rows)
        own = far_a if part == 0 else far_c
        there = (B, D1, D2)[part]
        for mat in (1, 2, 0):
            if part == 0:
                loads[mat].wait()
                if mat == 1:
                    loads[0].start()
            y = jnp.dot(
                nrm[nslot, src0 : src0 + rows, :], w_v[mat], preferred_element_type=jnp.float32
            )
            thirds = []
            for h in range(6):
                yh = y[:, h * DH : (h + 1) * DH]
                if mat != 2:
                    yh = yh * lax.rsqrt(jnp.mean(yh * yh, axis=-1, keepdims=True) + EPS)
                if mat == 0:
                    yh = yh * hs_ref[h] * (DH ** -0.5)
                thirds.append(yh.astype(jnp.bfloat16))
            for h in range(3):
                lanes = slice(h * DH, (h + 1) * DH)
                mine = jnp.where(zlo == 0, thirds[h], thirds[h + 3])
                theirs = jnp.where(zlo == 0, thirds[h + 3], thirds[h])
                if mat == 0:
                    qb[group_of[piece], rows_of[piece], lanes] = mine
                    st_q[st_rows, lanes] = theirs
                else:
                    own[0, frame(piece), mat - 1, rows_of[piece], lanes] = mine
                    st_kv[mat - 1, st_rows, lanes] = theirs
            if mat == 2:
                send(st_kv.at[:, st_rows], far_at(0, piece), inkv_s.at[part], inkv_r.at[part], inner)
                spread(piece)
            if mat == 0:
                send(st_q.at[st_rows], q_at(there), inq_s.at[part], inq_r.at[part], inner)

    def spread(piece):
        send(far_at(0, piece), near_at(1, piece), y_s.at[UP, piece], y_r.at[UP, piece], upper, has_up)
        send(far_at(0, piece), near_at(0, piece), y_s.at[DOWN, piece], y_r.at[DOWN, piece], lower, has_low)
        send(far_at(0, piece), far_at(0, piece), c0_s.at[piece], c0_r.at[piece], other)

    def from_inner(part, piece):
        recv(far_at(0, piece), inkv_s.at[part], inkv_r.at[part], inner)
        spread(piece)

    def pass_on(piece):
        recv(near_at(1, piece), y_s.at[UP, piece], y_r.at[UP, piece], upper, has_low)
        send(
            near_at(1, piece), far_at(2, piece), f_s.at[UP, piece], f_r.at[UP, piece], upper,
            has_up & has_low & (frame(piece) >= 1),
        )
        send(near_at(1, piece), near_at(1, piece), c1_s.at[UP, piece], c1_r.at[UP, piece], other, has_low)
        recv(near_at(0, piece), y_s.at[DOWN, piece], y_r.at[DOWN, piece], lower, has_up)
        send(
            near_at(0, piece), far_at(1, piece), f_s.at[DOWN, piece], f_r.at[DOWN, piece], lower,
            has_up & has_low & (frame(piece) <= 2),
        )
        send(near_at(0, piece), near_at(0, piece), c1_s.at[DOWN, piece], c1_r.at[DOWN, piece], other, has_up)

    from_up2, from_low2 = col < COLS - 2, col > 1

    def share_far(piece):
        when = from_low2 & (frame(piece) >= 1)
        recv(far_at(2, piece), f_s.at[UP, piece], f_r.at[UP, piece], upper, when)
        send(far_at(2, piece), far_at(2, piece), c2_s.at[UP, piece], c2_r.at[UP, piece], other, when)
        when = from_up2 & (frame(piece) <= 2)
        recv(far_at(1, piece), f_s.at[DOWN, piece], f_r.at[DOWN, piece], lower, when)
        send(far_at(1, piece), far_at(1, piece), c2_s.at[DOWN, piece], c2_r.at[DOWN, piece], other, when)

    j = core + 2 * zlo
    w_rows = 192 // WSUB

    def quarter(half, which, sub):
        return pl.ds(pl.multiple_of(half * 768 + which * 192 + sub * w_rows, 16), w_rows)

    other_j, inner_j = j + 1 - 2 * core, j + 2 - 4 * zlo
    diag_j = 3 - j

    def wo_cut(sub):
        src = pl.ds(pl.multiple_of(inner_j * 192 + sub * w_rows, 16), w_rows)
        send(wo_hbm.at[src], wo_v.at[quarter(t, inner_j, sub)], wc_s.at[sub], wc_r.at[sub], cut)

    def wo_share(sub):
        mine = wo_v.at[quarter(1 - t, j, sub)]
        recv(mine, wc_s.at[sub], wc_r.at[sub], cut)
        send(mine, mine, wi_s.at[sub], wi_r.at[sub], inner)
        send(mine, mine, wk_s.at[sub], wk_r.at[sub], other)

    def wo_second(sub):
        theirs = wo_v.at[quarter(1 - t, inner_j, sub)]
        recv(theirs, wi_s.at[sub], wi_r.at[sub], inner)
        send(theirs, theirs, wj_s.at[sub], wj_r.at[sub], other)

    def wo_last(sub):
        recv(wo_v.at[quarter(1 - t, other_j, sub)], wk_s.at[sub], wk_r.at[sub], other)
        recv(wo_v.at[quarter(1 - t, diag_j, sub)], wj_s.at[sub], wj_r.at[sub], other)

    project(0, 0, 0, 256, A)
    first_normed.wait_send()
    send_normed(1)
    wo_load.start()

    @pl.when(col == COLS - 1)
    def _():
        near_a[0] = jnp.zeros_like(near_a[0])
        near_c[0] = jnp.zeros_like(near_c[0])

    @pl.when(col == 0)
    def _():
        near_a[1] = jnp.zeros_like(near_a[1])
        near_c[1] = jnp.zeros_like(near_c[1])

    @pl.when(col >= COLS - 2)
    def _():
        far_a[1] = jnp.zeros_like(far_a[1])
        far_c[1] = jnp.zeros_like(far_c[1])

    @pl.when(col <= 1)
    def _():
        far_a[2] = jnp.zeros_like(far_a[2])
        far_c[2] = jnp.zeros_like(far_c[2])

    def place_of(unit):
        group, h = unit // 3, lax.rem(unit, 3)
        slot = jnp.where(group < 2, 1 - zlo, zlo)
        return group, slot, pl.ds(pl.multiple_of(h * DH, DH), DH)

    def near_blocks(slot, ref, own):
        mine = core + 2 * slot
        o = jnp.where(slot == zlo, off_ref[0], offs[0])
        blocks = [(own, (0, mine), None)]
        for i in range(4):
            below = 4 + i - mine > WIN - 1 - o
            side = jnp.where(below, 1, 0)
            blocks.append((ref, (side, i), jnp.where(below, has_low, has_up)))
        return blocks

    def far_blocks(slot, ref):
        mine = core + 2 * slot
        o = jnp.where(slot == zlo, off_ref[0], offs[0])
        blocks = []
        for n in range(3):
            r = n + jnp.where(n >= mine, 1, 0)
            less = r < mine
            inside = jnp.where(less, mine - r <= o, r - mine <= WIN - 1 - o)
            side = jnp.where(inside, 0, jnp.where(less, 1, 2))
            blocks.append((ref, (side, r), inside | jnp.where(less, from_up2, from_low2)))
        return blocks

    def stage_blocks(stage, slot):
        if stage == 0:
            return near_blocks(slot, near_a, far_a) + far_blocks(slot, far_a)
        if stage == 1:
            return near_blocks(slot, near_c, far_c)
        return far_blocks(slot, far_c)

    COUNT = (8, 5, 3)

    def score(stage, unit, b, buf, top):
        group, slot, lanes = place_of(unit)
        ref, lead, valid = stage_blocks(stage, slot)[b]
        s = lax.dot_general(
            qb[group, :, lanes], ref[(*lead, 0, slice(None), lanes)],
            (((1,), (1,)), ((), ())), preferred_element_type=jnp.float32,
        )
        buf[:, b * HALF : (b + 1) * HALF] = s
        high = jnp.maximum(s[:, :DH], s[:, DH:])
        if valid is not None:
            high = jnp.where(valid, high, LOW)
        return high if top is None else jnp.maximum(top, high)

    def peak(stage, unit, top):
        high = jnp.broadcast_to(jnp.max(top, axis=1, keepdims=True), (HALF, DH))
        if stage > 0:
            before = m_s[unit]
            high = jnp.maximum(high, before)
            scale = jnp.exp(before - high)
            acc_s[unit] = acc_s[unit] * scale
            l_s[unit] = l_s[unit] * scale
        m_s[unit] = high

    def weigh(stage, unit, b, buf, high, total, weighted):
        _, slot, lanes = place_of(unit)
        ref, lead, valid = stage_blocks(stage, slot)[b]
        base = high if valid is None else jnp.where(valid, high, HIGH)
        p = [jnp.exp(buf[:, b * HALF + c * DH : b * HALF + (c + 1) * DH] - base) for c in range(2)]
        part = p[0] + p[1]
        rounded = jnp.concatenate([c.astype(jnp.bfloat16) for c in p], axis=1)
        o = jnp.dot(rounded, ref[(*lead, 1, slice(None), lanes)], preferred_element_type=jnp.float32)
        return (part if total is None else total + part), (o if weighted is None else weighted + o)

    def finish(stage, unit, total, weighted):
        if stage > 0:
            total = total + l_s[unit]
            weighted = weighted + acc_s[unit]
        if stage < 2:
            l_s[unit] = total
            acc_s[unit] = weighted
        else:
            group, _, lanes = place_of(unit)
            ob[group, :, lanes] = (weighted / jnp.sum(total, axis=1, keepdims=True)).astype(jnp.bfloat16)

    def start_unit(stage, unit, buf):
        top = None
        for b in range(COUNT[stage]):
            top = score(stage, unit, b, buf, top)
        peak(stage, unit, top)

    def step(stage, unit, buf, following, other_buf):
        high = m_s[unit]
        top = total = weighted = None
        for b in range(COUNT[stage]):
            if following is not None:
                top = score(stage, following, b, other_buf, top)
            total, weighted = weigh(stage, unit, b, buf, high, total, weighted)
        finish(stage, unit, total, weighted)
        if following is not None:
            peak(stage, following, top)

    def units(stage, low, high):
        start_unit(stage, low, even)

        def two(i, carry):
            unit = low + 2 * i
            step(stage, unit, even, unit + 1, odd)
            step(stage, unit + 1, odd, jnp.minimum(unit + 2, high - 1), even)
            return carry

        lax.fori_loop(0, (high - low) // 2, two, 0)

    def near_from_core(*pieces):
        for piece in pieces:
            recv(near_at(1, piece, 1 - core), c1_s.at[UP, piece], c1_r.at[UP, piece], other, has_low)
            recv(near_at(0, piece, 1 - core), c1_s.at[DOWN, piece], c1_r.at[DOWN, piece], other, has_up)

    def own_from_core(*pieces):
        for piece in pieces:
            recv(far_at(0, piece, 1 - core), c0_s.at[piece], c0_r.at[piece], other)

    def far_from_core(*pieces):
        for piece in pieces:
            recv(
                far_at(2, piece, 1 - core), c2_s.at[UP, piece], c2_r.at[UP, piece], other,
                from_low2 & (frame(piece, 1 - core) >= 1),
            )
            recv(
                far_at(1, piece, 1 - core), c2_s.at[DOWN, piece], c2_r.at[DOWN, piece], other,
                from_up2 & (frame(piece, 1 - core) <= 2),
            )

    from_inner(0, B)
    pass_on(A)
    recv(nrm.at[1, pl.ds(0, 128)], cut_s.at[0], cut_r.at[0], cut)
    project(1, 1, 0, 128, C1)
    pass_on(B)
    from_inner(1, D1)
    recv(nrm.at[1, pl.ds(128, 128)], cut_s.at[1], cut_r.at[1], cut)
    for sub in range(WSUB):
        wo_cut(sub)
    project(2, 1, 128, 128, C2)
    pass_on(C1)
    pass_on(D1)
    from_inner(2, D2)
    share_far(A)
    share_far(B)
    wo_share(0)
    recv(offs, off_sem.at[0], off_sem.at[1], inner)
    for part, piece in ((0, B), (1, D1), (2, D2)):
        recv(q_at(piece), inq_s.at[part], inq_r.at[part], inner)
    near_from_core(A, B)
    own_from_core(A, B)
    far_from_core(A, B)
    units(0, 0, 6)
    pass_on(C2)
    wo_share(1)
    wo_second(0)
    units(0, 6, 12)
    pass_on(D2)
    share_far(C1)
    share_far(D1)
    wo_share(2)
    wo_second(1)
    near_from_core(C1, D1, C2, D2)
    own_from_core(C1, D1, C2, D2)
    units(1, 0, 6)
    wo_share(3)
    wo_second(2)
    units(1, 6, 12)
    share_far(C2)
    share_far(D2)
    wo_second(3)
    far_from_core(C1, D1, C2, D2)

    triple = 2 * t + zlo
    goes_to = (inner, cut, peer)
    start_unit(2, 0, even)
    for unit in range(12):
        bufs = (even, odd) if unit % 2 == 0 else (odd, even)
        step(2, unit, bufs[0], unit + 1 if unit < 11 else None, bufs[1])
        if unit % 3 == 2 and unit < 9:
            n = unit // 3
            send(ob.at[n], att.at[triple], o_s.at[n], o_r.at[n], goes_to[n])
    att[triple] = ob[3]

    def joined(half):
        return jnp.concatenate([att[2 * half], att[2 * half + 1]], axis=1)

    def out_rows(half):
        return pl.ds(pl.multiple_of(half * 768, 768), 768)

    wo_load.wait()
    recv(att.at[2 * t + 1 - zlo], o_s.at[0], o_r.at[0], inner)
    left = joined(t)
    for n in range(D // 512):
        buf, at = (even, n * 512) if n < 4 else (odd, (n - 4) * 512)
        buf[:, at : at + 512] = jnp.dot(
            left, wo_v[out_rows(t), n * 512 : (n + 1) * 512], preferred_element_type=jnp.float32
        )
    for sub in range(WSUB):
        wo_last(sub)
    recv(att.at[2 * (1 - t) + 1 - zlo], o_s.at[1], o_r.at[1], cut)
    recv(att.at[2 * (1 - t) + zlo], o_s.at[2], o_r.at[2], peer)
    right = joined(1 - t)
    for n in range(D // 512):
        buf, at = (even, n * 512) if n < 4 else (odd, (n - 4) * 512)
        lanes = slice(n * 512, (n + 1) * 512)
        branch = buf[:, at : at + 512] + jnp.dot(
            right, wo_v[out_rows(1 - t), lanes], preferred_element_type=jnp.float32
        )
        x = x_ref[0, :, lanes].astype(jnp.float32)
        out_ref[0, :, lanes] = (x + mod_ref[2:3, lanes] * branch).astype(jnp.bfloat16)
    for copy, when in pending:
        if when is None:
            copy.wait_send()
        else:
            pl.when(when)(copy.wait_send)


def shards(latents, levels, offsets, level_table, w_qkv, w_out, head_scale):
    table = jnp.transpose(level_table, (1, 0, 2))
    modulation = lax.dynamic_index_in_dim(table, levels[0], 1, keepdims=False)
    weights = jnp.transpose(w_qkv, (1, 0, 2))
    bf, f32 = jnp.bfloat16, jnp.float32
    dma = pltpu.SemaphoreType.DMA
    vmem = pl.BlockSpec(memory_space=pltpu.VMEM)
    smem = pl.BlockSpec(memory_space=pltpu.SMEM)
    hbm = pl.BlockSpec(memory_space=pl.ANY)
    pair = lambda *n: [dma(n), dma(n)]
    return pl.pallas_call(
        body,
        out_shape=jax.ShapeDtypeStruct((1, HALF, D), bf),
        in_specs=[vmem, vmem, hbm, hbm, smem, smem],
        out_specs=vmem,
        scratch_shapes=[
            pltpu.VMEM((2, 4, 2, HALF, TRI), bf),
            pltpu.VMEM((2, 4, 2, HALF, TRI), bf),
            pltpu.VMEM((3, 4, 2, HALF, TRI), bf),
            pltpu.VMEM((3, 4, 2, HALF, TRI), bf),
            pltpu.VMEM((4, HALF, TRI), bf),
            pltpu.VMEM((3, D, 768), bf),
            pltpu.VMEM((1536, D), bf),
            pltpu.VMEM((2, HALF, D), bf),
            pltpu.VMEM((2, TOK, TRI), bf),
            pltpu.VMEM((TOK, TRI), bf),
            pltpu.VMEM((HALF, 8 * HALF), f32),
            pltpu.VMEM((HALF, 8 * HALF), f32),
            pltpu.VMEM((12, HALF, DH), f32),
            pltpu.VMEM((12, HALF, DH), f32),
            pltpu.VMEM((12, HALF, DH), f32),
            pltpu.VMEM((4, HALF, TRI), bf),
            pltpu.VMEM((4, HALF, TRI), bf),
            pltpu.SMEM((1,), jnp.int32),
            dma((4,)), dma((2,)),
            *pair(2), *pair(3), *pair(3), *pair(2, 6), *pair(2, 6),
            *pair(6), *pair(2, 6), *pair(2, 6),
            *pair(WSUB), *pair(WSUB), *pair(WSUB), *pair(WSUB), *pair(3),
        ],
        compiler_params=pltpu.CompilerParams(
            collective_id=0, has_side_effects=True, vmem_limit_bytes=62 * 2**20
        ),
        cost_estimate=pl.CostEstimate(flops=17 * 10**9, bytes_accessed=25 * 10**6, transcendentals=13 * 10**6),
        name="frame_attention",
    )(latents, modulation, weights, w_out, offsets, head_scale)


def solution(mesh):
    placed = (
        P("queue", "tok", None),
        P("queue"),
        P("queue"),
        P(),
        P(None, None, "tok"),
        P("tok", None),
        P("tok"),
    )
    return jax.shard_map(
        shards, mesh=mesh, in_specs=placed, out_specs=P("queue", "tok", None), check_vma=False
    )
```

time: 121 us -> 112 us (0.926)
  Pallas kernels: 116 us -> 106 us
    pallas_call x1, Pallas kernels: 116 us -> 106 us  [shards(): pl.pallas_call(body, out_shape=jax.ShapeDtypeStruct((1, HALF, D), bf), in...]
where the time goes in v2:
time: 112 us; the launch traced here: 111 us
  Pallas kernels  106 us (95%)
  local copies, waits for them, and re-layouts  4.28 us (4%)
  between operations  1.31 us (1%)
    pallas_call x1, Pallas kernels, shards(): pl.pallas_call(body, out_shape=jax.ShapeDtypeStruct((1, HALF, D), bf), in...  106 us
    unnamed x2, local copies, waits for them, and re-layouts  3.29 us

profile of v2, /device:TPU:1, one launch (start us, length us, event | category | flops | bytes accessed | tf_op | source)
XLA Modules:
  0.0 111.5 jit_solution(4656211784915101874)
XLA Ops:
  1.3 1.0 constant_dynamic-slice_fusion
  2.3 0.6 copy.10
  2.9 105.9 %frame_attention.1 = bf16[1,256,3072]{2,1,0:T(8,128)(2,1)} custom-call(bf16[1,256,3072]{2,1,0:T(8,128)(2,1)} %x_ref.1, f32[3,3072]{1,0:T(4,128)} %bitcast.8, bf16[3,3072,768]{2,1,0:T(8,128)(2,1)} %bitcast.9, bf16[768,3072]{1,0:T(8,128)(2,1)} %wo_hbm.1, s32[1]{0:T(128)S(6)} %copy.13.off_ref, f32[6]{0:T(128)} %hs_ref.1), custom_call_target="tpu_custom_call" | custom-call | flops 16999999488 | bytes 25000000 | tf_op jit(solution)/shard_map/frame_attention/pallas_call | solution.py:474
  108.8 2.7 %copy.14 = bf16[1,256,3072]{2,1,0:T(8,128)(2,1)} copy(bf16[1,256,3072]{2,1,0:T(8,128)(2,1)} %frame_attention.1) | data formatting | bytes 3145728

commit v3 on v2

--- a/solution.py
+++ b/solution.py
@@ -103,7 +103,7 @@
     send(off_ref, offs, off_sem.at[0], off_sem.at[1], inner)
 
     slot_of = {A: zlo, B: 1 - zlo, C1: 1 - zlo, D1: zlo, C2: 1 - zlo, D2: zlo}
-    group_of = {A: 3, B: 0, C1: 1, D1: 2, C2: 1, D2: 2}
+    group_of = {A: 0, B: 1, C1: 2, D1: 3, C2: 2, D2: 3}
     rows_of = {
         A: pl.ds(0, 256), B: pl.ds(0, 256), C1: pl.ds(0, 128), D1: pl.ds(0, 128),
         C2: pl.ds(128, 128), D2: pl.ds(128, 128),
@@ -247,7 +247,7 @@
 
     def place_of(unit):
         group, h = unit // 3, lax.rem(unit, 3)
-        slot = jnp.where(group < 2, 1 - zlo, zlo)
+        slot = jnp.where((group == 0) | (group == 3), zlo, 1 - zlo)
         return group, slot, pl.ds(pl.multiple_of(h * DH, DH), DH)
 
     def near_blocks(slot, ref, own):
@@ -274,12 +274,14 @@
 
     def stage_blocks(stage, slot):
         if stage == 0:
-            return near_blocks(slot, near_a, far_a) + far_blocks(slot, far_a)
+            return near_blocks(slot, near_a, far_a)
         if stage == 1:
+            return far_blocks(slot, far_a)
+        if stage == 2:
             return near_blocks(slot, near_c, far_c)
         return far_blocks(slot, far_c)
 
-    COUNT = (8, 5, 3)
+    COUNT = (5, 3, 5, 3)
 
     def score(stage, unit, b, buf, top):
         group, slot, lanes = place_of(unit)
@@ -318,7 +320,7 @@
         if stage > 0:
             total = total + l_s[unit]
             weighted = weighted + acc_s[unit]
-        if stage < 2:
+        if stage < 3:
             l_s[unit] = total
             acc_s[unit] = weighted
         else:
@@ -379,53 +381,59 @@
     project(1, 1, 0, 128, C1)
     pass_on(B)
     from_inner(1, D1)
+    recv(offs, off_sem.at[0], off_sem.at[1], inner)
+    recv(q_at(B), inq_s.at[0], inq_r.at[0], inner)
+    near_from_core(A, B)
+    own_from_core(A, B)
+    units(0, 0, 6)
     recv(nrm.at[1, pl.ds(128, 128)], cut_s.at[1], cut_r.at[1], cut)
-    for sub in range(WSUB):
-        wo_cut(sub)
+    wo_cut(0)
+    wo_cut(1)
     project(2, 1, 128, 128, C2)
+    from_inner(2, D2)
+    wo_cut(2)
+    wo_cut(3)
+    recv(q_at(D1), inq_s.at[1], inq_r.at[1], inner)
+    recv(q_at(D2), inq_s.at[2], inq_r.at[2], inner)
+    units(0, 6, 12)
     pass_on(C1)
     pass_on(D1)
-    from_inner(2, D2)
+    pass_on(C2)
+    wo_share(0)
+    wo_share(1)
     share_far(A)
     share_far(B)
-    wo_share(0)
-    recv(offs, off_sem.at[0], off_sem.at[1], inner)
-    for part, piece in ((0, B), (1, D1), (2, D2)):
-        recv(q_at(piece), inq_s.at[part], inq_r.at[part], inner)
-    near_from_core(A, B)
-    own_from_core(A, B)
     far_from_core(A, B)
-    units(0, 0, 6)
-    pass_on(C2)
-    wo_share(1)
-    wo_second(0)
-    units(0, 6, 12)
+    units(1, 0, 6)
     pass_on(D2)
+    units(1, 6, 12)
+    wo_share(2)
+    wo_share(3)
     share_far(C1)
     share_far(D1)
-    wo_share(2)
-    wo_second(1)
     near_from_core(C1, D1, C2, D2)
     own_from_core(C1, D1, C2, D2)
-    units(1, 0, 6)
-    wo_share(3)
-    wo_second(2)
-    units(1, 6, 12)
+    units(2, 0, 6)
+    wo_second(0)
+    wo_second(1)
+    units(2, 6, 12)
     share_far(C2)
     share_far(D2)
+    far_from_core(C1, D1, C2, D2)
+
+    triple = 2 * t + zlo
+    goes_to = (None, inner, cut, peer)
+    order = (3, 4, 5, 6, 7, 8, 9, 10, 11, 0, 1, 2)
+    start_unit(3, order[0], even)
+    for n, unit in enumerate(order):
+        bufs = (even, odd) if n % 2 == 0 else (odd, even)
+        step(3, unit, bufs[0], order[n + 1] if n < 11 else None, bufs[1])
+        group = unit // 3
+        if unit % 3 == 2 and group > 0:
+            send(ob.at[group], att.at[triple], o_s.at[group - 1], o_r.at[group - 1], goes_to[group])
+    att[triple] = ob[0]
+    wo_second(2)
     wo_second(3)
-    far_from_core(C1, D1, C2, D2)
-
-    triple = 2 * t + zlo
-    goes_to = (inner, cut, peer)
-    start_unit(2, 0, even)
-    for unit in range(12):
-        bufs = (even, odd) if unit % 2 == 0 else (odd, even)
-        step(2, unit, bufs[0], unit + 1 if unit < 11 else None, bufs[1])
-        if unit % 3 == 2 and unit < 9:
-            n = unit // 3
-            send(ob.at[n], att.at[triple], o_s.at[n], o_r.at[n], goes_to[n])
-    att[triple] = ob[3]
 
     def joined(half):
         return jnp.concatenate([att[2 * half], att[2 * half + 1]], axis=1)
@@ -437,7 +445,7 @@
     recv(att.at[2 * t + 1 - zlo], o_s.at[0], o_r.at[0], inner)
     left = joined(t)
     for n in range(D // 512):
-        buf, at = (even, n * 512) if n < 4 else (odd, (n - 4) * 512)
+        buf, at = (even, n * 512) if n < 3 else (odd, (n - 3) * 512)
         buf[:, at : at + 512] = jnp.dot(
             left, wo_v[out_rows(t), n * 512 : (n + 1) * 512], preferred_element_type=jnp.float32
         )
@@ -447,7 +455,7 @@
     recv(att.at[2 * (1 - t) + zlo], o_s.at[2], o_r.at[2], peer)
     right = joined(1 - t)
     for n in range(D // 512):
-        buf, at = (even, n * 512) if n < 4 else (odd, (n - 4) * 512)
+        buf, at = (even, n * 512) if n < 3 else (odd, (n - 3) * 512)
         lanes = slice(n * 512, (n + 1) * 512)
         branch = buf[:, at : at + 512] + jnp.dot(
             right, wo_v[out_rows(1 - t), lanes], preferred_element_type=jnp.float32
@@ -487,8 +495,8 @@
             pltpu.VMEM((2, HALF, D), bf),
             pltpu.VMEM((2, TOK, TRI), bf),
             pltpu.VMEM((TOK, TRI), bf),
-            pltpu.VMEM((HALF, 8 * HALF), f32),
-            pltpu.VMEM((HALF, 8 * HALF), f32),
+            pltpu.VMEM((HALF, D // 2), f32),
+            pltpu.VMEM((HALF, D // 2), f32),
             pltpu.VMEM((12, HALF, DH), f32),
             pltpu.VMEM((12, HALF, DH), f32),
             pltpu.VMEM((12, HALF, DH), f32),

time: 112 us -> 107 us (0.955); the launches traced: 111 us -> 105 us
  Pallas kernels: 106 us -> 99.6 us
    pallas_call x1, Pallas kernels: 106 us -> 99.6 us  [shards(): pl.pallas_call(body, out_shape=jax.ShapeDtypeStruct((1, HALF, D), bf), in...]
where the time goes in v3:
time: 107 us; the launch traced here: 105 us
  Pallas kernels  99.6 us (93%)
  local copies, waits for them, and re-layouts  4.28 us (4%)
  between operations  1.31 us (1%)
    pallas_call x1, Pallas kernels, shards(): pl.pallas_call(body, out_shape=jax.ShapeDtypeStruct((1, HALF, D), bf), in...  99.6 us
    unnamed x2, local copies, waits for them, and re-layouts  3.29 us

profile of v3, /device:TPU:1, one launch (start us, length us, event | category | flops | bytes accessed | tf_op | source)
XLA Modules:
  0.0 105.2 jit_solution(14048633227126886596)
XLA Ops:
  1.3 1.0 constant_dynamic-slice_fusion
  2.3 0.6 copy.10
  2.9 99.6 %frame_attention.1 = bf16[1,256,3072]{2,1,0:T(8,128)(2,1)} custom-call(bf16[1,256,3072]{2,1,0:T(8,128)(2,1)} %x_ref.1, f32[3,3072]{1,0:T(4,128)} %bitcast.8, bf16[3,3072,768]{2,1,0:T(8,128)(2,1)} %bitcast.9, bf16[768,3072]{1,0:T(8,128)(2,1)} %wo_hbm.1, s32[1]{0:T(128)S(6)} %copy.13.off_ref, f32[6]{0:T(128)} %hs_ref.1), custom_call_target="tpu_custom_call" | custom-call | flops 16999999488 | bytes 25000000 | tf_op jit(solution)/shard_map/frame_attention/pallas_call | solution.py:482
  102.5 2.7 %copy.14 = bf16[1,256,3072]{2,1,0:T(8,128)(2,1)} copy(bf16[1,256,3072]{2,1,0:T(8,128)(2,1)} %frame_attention.1) | data formatting | bytes 3145728

commit v4 on v3

--- a/solution.py
+++ b/solution.py
@@ -396,19 +396,19 @@
     recv(q_at(D1), inq_s.at[1], inq_r.at[1], inner)
     recv(q_at(D2), inq_s.at[2], inq_r.at[2], inner)
     units(0, 6, 12)
+    wo_share(0)
+    wo_share(1)
     pass_on(C1)
     pass_on(D1)
     pass_on(C2)
-    wo_share(0)
-    wo_share(1)
     share_far(A)
     share_far(B)
     far_from_core(A, B)
     units(1, 0, 6)
     pass_on(D2)
-    units(1, 6, 12)
     wo_share(2)
     wo_share(3)
+    units(1, 6, 12)
     share_far(C1)
     share_far(D1)
     near_from_core(C1, D1, C2, D2)

time: 107 us -> 107 us (level)
  no operation moved by 1% of the time
where the time goes in v4:
time: 107 us; the launch traced here: 106 us
  Pallas kernels  99.9 us (93%)
  local copies, waits for them, and re-layouts  4.28 us (4%)
  between operations  1.31 us (1%)
    pallas_call x1, Pallas kernels, shards(): pl.pallas_call(body, out_shape=jax.ShapeDtypeStruct((1, HALF, D), bf), in...  99.9 us
    unnamed x2, local copies, waits for them, and re-layouts  3.29 us

profile of v4, /device:TPU:1, one launch (start us, length us, event | category | flops | bytes accessed | tf_op | source)
XLA Modules:
  0.0 105.5 jit_solution(100924811722760485)
XLA Ops:
  1.3 1.0 constant_dynamic-slice_fusion
  2.3 0.6 copy.10
  2.9 99.9 %frame_attention.1 = bf16[1,256,3072]{2,1,0:T(8,128)(2,1)} custom-call(bf16[1,256,3072]{2,1,0:T(8,128)(2,1)} %x_ref.1, f32[3,3072]{1,0:T(4,128)} %bitcast.8, bf16[3,3072,768]{2,1,0:T(8,128)(2,1)} %bitcast.9, bf16[768,3072]{1,0:T(8,128)(2,1)} %wo_hbm.1, s32[1]{0:T(128)S(6)} %copy.13.off_ref, f32[6]{0:T(128)} %hs_ref.1), custom_call_target="tpu_custom_call" | custom-call | flops 16999999488 | bytes 25000000 | tf_op jit(solution)/shard_map/frame_attention/pallas_call | solution.py:482
  102.9 2.7 %copy.14 = bf16[1,256,3072]{2,1,0:T(8,128)(2,1)} copy(bf16[1,256,3072]{2,1,0:T(8,128)(2,1)} %frame_attention.1) | data formatting | bytes 3145728
